TPU v7x, 32 devices: a whole 2x2x4 slice. The times are simulated.
32 devices in a mesh: groups: 2 (over x), seq: 8 (over z, y), tp: 2 (over core).
Axes of the slice: x: 2, y: 2, z: 4, core: 2. Of those that a mesh axis runs over, the one named last changes fastest.
Arguments:
- queries: bfloat16 [16384, 4096], P(('groups', 'seq'), 'tp'), parts along dimension 0, may hold values from -6 to 6
- keys: bfloat16 [16384, 4096], P(('groups', 'seq'), 'tp'), parts along dimension 0, may hold values from -6 to 6
- values: bfloat16 [16384, 4096], P(('groups', 'seq'), 'tp'), parts along dimension 0, may hold values from -6 to 6
- log_decay: float32 [16384, 32], P(('groups', 'seq'), 'tp'), parts along dimension 0, may hold values from -1 to 0, as said below
- gate: bfloat16 [16384, 4096], P(('groups', 'seq'), 'tp'), parts along dimension 0, may hold values from -6 to 6
- gain: bfloat16 [4096], P('tp'), may hold values from 0.099609375 to 1.8984375
- doc_lengths: int32 [16], P('groups'), parts along dimension 0, may hold values from 1 to 4096, 8192 in all
- owner_ids: int32 [16], P('groups'), parts along dimension 0, may hold values from 0 to 7, each once
Outputs:
- mixed: bfloat16 [16384, 4096], P(('groups', 'seq'), 'tp'), parts along dimension 0
- owner_states: bfloat16 [16, 32, 128, 128], P(('groups', 'seq'), 'tp'), parts along dimension 0
There are 2 independent parts, one for each index of `groups`. A program takes and returns all parts, laid end to end along the dimension named above; an argument that names none is the same for every part. Nothing has to cross between parts.
Inputs may be any that keep to these rules, and one draw needn't show every extreme that they name: `doc_lengths`: positive lengths summing to 8192; the longest prompt has exactly 4096 tokens. `owner_ids`: a permutation of the owner slots. `log_decay`: negative.
All inputs are finite; a program needn't handle non-finite values.
Results may differ from a plain program's by a relative error of at most 0.0049.
Values may be sent and summed in bfloat16 or wider, within the bound.
No kernel may reach another device: no remote copies, remote signals or barrier semaphores. Data moves between devices by JAX's collectives and lax.ppermute only.
A program may use at most 192 MiB of HBM per device.

v0:
```python
import functools
import math

import jax
import jax.numpy as jnp
from jax import lax
from jax.experimental import pallas as pl
from jax.experimental.pallas import tpu as pltpu
from jax.sharding import PartitionSpec as P

BLK = 512
SIDE = 3
EXTRA = 16
CHUNK = 256
MEMBERS = 4
NEG = -1e30
LOG2E = math.log2(math.e)
SCALE = 128**-0.5
F32, BF16 = jnp.float32, jnp.bfloat16
SMEM = pl.BlockSpec(memory_space=pltpu.SMEM)
VMEM = pl.BlockSpec(memory_space=pltpu.VMEM)
LIMIT = pltpu.CompilerParams(vmem_limit_bytes=60 * 2**20)
SMALL = pltpu.CompilerParams(vmem_limit_bytes=48 * 2**20)


def dot(a, b, contract=((1,), (0,))):
    return lax.dot_general(a, b, (contract, ((), ())), preferred_element_type=F32)


def iota(shape, dim):
    return lax.broadcasted_iota(jnp.int32, shape, dim)


def read_ends(len_ref, count):
    ends, total = [], jnp.int32(0)
    for d in range(count):
        total = total + len_ref[d]
        ends.append(total)
    return ends


def run_end(ends, pos):
    best = ends[-1]
    for e in reversed(ends[:-1]):
        best = jnp.where(e > pos, e, best)
    return best


def run_start(ends, pos):
    best = jnp.zeros_like(pos)
    for e in ends[:-1]:
        best = jnp.where(e <= pos, e, best)
    return best


def split3(x):
    hi = x.astype(BF16)
    rest = x - hi.astype(F32)
    mid = rest.astype(BF16)
    return hi, mid, (rest - mid.astype(F32)).astype(BF16)


def cum_rows(ld_ref, crow_ref):
    heads, rows = ld_ref.shape
    upper = (iota((BLK, BLK), 0) <= iota((BLK, BLK), 1)).astype(F32).astype(BF16)
    base = jnp.zeros((heads, 1), F32)
    for b in range(rows // BLK):
        part = ld_ref[:, b * BLK : (b + 1) * BLK] * LOG2E
        sums = dot(jnp.concatenate(split3(part), axis=0), upper)
        row = sums[2 * heads :] + sums[heads : 2 * heads] + sums[:heads] + base
        crow_ref[:, b * BLK : (b + 1) * BLK] = row
        base = row[:, BLK - 1 :]


def value_at(cum, at, index):
    return jnp.sum(jnp.where(at == index, cum, 0.0), axis=1, keepdims=True)


def span_weights(cum, at, low, high):
    inside = (at >= low) & (at <= high)
    return jnp.exp2(jnp.where(inside, value_at(cum, at, high) - cum, NEG) + math.log2(SCALE))


def weigh(flipped, w_ref, h):
    weights = [jnp.broadcast_to(w_ref[pl.ds(h + j, 1), :], (128, flipped.shape[1])) for j in range(2)]
    return (flipped.astype(F32) * jnp.concatenate(weights, axis=0)).astype(BF16)


def whole(shape):
    return pl.BlockSpec(shape, lambda j: (0,) * len(shape))


def pieces_kernel(by_owner, len_ref, own_ref, ld_ref, k_ref, v_ref, *refs):
    if by_owner:
        side_ref, crow_ref, w_ref, keep_ref = refs
    else:
        side_ref, crow_ref, flag_ref = refs[:3]
        last_refs = refs[3 : 3 + MEMBERS]
        w_ref, keep_ref, first_ref = refs[3 + MEMBERS :]
    heads, rows = crow_ref.shape
    slots = keep_ref.shape[0]
    step = pl.program_id(0)
    hp = v_ref.shape[1] // 128
    me = lax.axis_index("seq")

    @pl.when(step == 0)
    def _():
        cum_rows(ld_ref, crow_ref)
        first = me * rows
        last = first + rows - 1
        ends = read_ends(len_ref, len_ref.shape[0])
        starts = [jnp.int32(0)] + ends[:-1]
        lows = [jnp.int32(0)] * slots
        highs = [jnp.int32(-1)] * slots
        place, rank, previous = jnp.int32(0), jnp.int32(0), jnp.int32(-1)
        crowded, owned_in, owned_late = jnp.int32(0), jnp.int32(0), jnp.int32(0)
        for d in range(len(ends)):
            here = (ends[d] > first) & (ends[d] <= last)
            low = jnp.maximum(starts[d] - first, 0)
            for s in range(slots):
                mine = here & ((place >= SIDE) & (own_ref[d] == s) if by_owner else (place == s))
                lows[s] = jnp.where(mine, low, lows[s])
                highs[s] = jnp.where(mine, ends[d] - 1 - first, highs[s])
            place = place + here.astype(jnp.int32)
            device = (ends[d] - 1) // rows
            rank = jnp.where(device == previous, rank + 1, 0)
            previous = device
            late = ((rank >= SIDE) & (ends[d] != (device + 1) * rows)).astype(jnp.int32)
            crowded = jnp.maximum(crowded, late)
            owned_in = jnp.where(own_ref[d] == me, device, owned_in)
            owned_late = jnp.where(own_ref[d] == me, late, owned_late)
        if not by_owner:
            lows[SIDE] = jnp.maximum(run_start(ends, last) - first, 0)
            highs[SIDE] = jnp.int32(rows - 1)
            flag_ref[0] = owned_in // MEMBERS
            flag_ref[1] = owned_late
            flag_ref[2] = crowded
            flag_ref[3] = owned_in
        at = iota((heads, rows), 1)
        cum = crow_ref[...]
        row_at = iota((16, rows), 1)
        total = jnp.zeros((heads, rows), F32)
        for s in range(slots):
            total = total + span_weights(cum, at, lows[s], highs[s])
            inside = (row_at >= lows[s]) & (row_at <= highs[s])
            keep_ref[s] = jnp.where(inside, 1.0, 0.0).astype(BF16)
        w_ref[...] = total
        if not by_owner:
            stop = jnp.minimum(run_end(ends, first) - 1 - first, rows - 1)
            goes_on = (run_start(ends, first) < first).astype(F32)
            first_ref[...] = jnp.broadcast_to(jnp.exp2(value_at(cum, at, stop)) * goes_on, (heads, 128))

    weighted = []
    for i in range(0, hp, 2):
        flipped = k_ref[:, i * 128 : (i + 2) * 128].T
        weighted.append(weigh(flipped, w_ref, step * hp + i).reshape(16, 16, rows))
    last_states = []
    for i in range(0, hp, 2):
        value = v_ref[:, i * 128 : (i + 2) * 128]
        for s in range(slots):
            kept = (weighted[i // 2] * keep_ref[s][None]).reshape(256, rows)
            states = dot(kept, value)
            for j in range(2):
                state = states[j * 128 : (j + 1) * 128, j * 128 : (j + 1) * 128].astype(BF16)
                if by_owner:
                    side_ref[s, i + j] = state
                elif s < SIDE:
                    at = (s * hp + i + j) * 128
                    side_ref[0, at : at + 128, :] = state
                else:
                    last_states.append(state)
    if not by_owner:
        rate = first_ref[pl.ds(step * hp, hp), :]
        high = rate.astype(BF16).astype(F32)
        pad = jnp.zeros((EXTRA - 2 * hp, 128), F32)
        tail = jnp.concatenate([high, rate - high, pad], axis=0).astype(BF16)
        for x, last_ref in enumerate(last_refs):

            @pl.when((step ^ (me % MEMBERS)) == x)
            def _():
                for i in range(hp):
                    last_ref[i * 128 : (i + 1) * 128, :] = last_states[i]
                last_ref[hp * 128 :, :] = tail


def piece_states(doc_lengths, owner_ids, decay_rows, keys, values, spread=0):
    heads, rows = decay_rows.shape
    by_owner = spread > 0
    hp = 2 if by_owner else heads // MEMBERS
    slots = spread if by_owner else SIDE + 1
    wide = pl.BlockSpec((rows, hp * 128), lambda j: (0, j))
    scratch = [pltpu.VMEM((heads, rows), F32), pltpu.VMEM((slots, 16, rows), BF16)]
    if by_owner:
        shapes = [jax.ShapeDtypeStruct((slots, heads, 128, 128), BF16), jax.ShapeDtypeStruct((heads, rows), F32)]
        specs = [pl.BlockSpec((slots, hp, 128, 128), lambda j: (0, j, 0, 0)), whole((heads, rows))]
    else:
        last = (hp * 128 + EXTRA, 128)
        shapes = [
            jax.ShapeDtypeStruct((MEMBERS, SIDE * hp * 128, 128), BF16),
            jax.ShapeDtypeStruct((heads, rows), F32),
            jax.ShapeDtypeStruct((4,), jnp.int32),
        ] + [jax.ShapeDtypeStruct(last, BF16)] * MEMBERS
        specs = [pl.BlockSpec((1, SIDE * hp * 128, 128), lambda j: (j, 0, 0)), whole((heads, rows)), SMEM]
        specs += [whole(last)] * MEMBERS
        scratch.append(pltpu.VMEM((heads, 128), F32))
    return pl.pallas_call(
        functools.partial(pieces_kernel, by_owner),
        grid=(heads // hp,),
        in_specs=[SMEM, SMEM, whole((heads, rows)), wide, wide],
        out_specs=specs,
        out_shape=shapes,
        scratch_shapes=scratch,
        compiler_params=LIMIT,
        cost_estimate=pl.CostEstimate(
            flops=slots * heads * rows * 128 * 256, bytes_accessed=rows * heads * 128 * 4, transcendentals=heads * rows
        ),
        name="piece_states",
    )(doc_lengths, owner_ids, decay_rows, keys, values)


def head_column(ccol_ref, h):
    cols = ccol_ref[...]
    return jnp.sum(jnp.where(iota(cols.shape, 1) == h, cols, 0.0), axis=1, keepdims=True)


def fill_columns(crow_ref, ccol_ref):
    heads, rows = crow_ref.shape
    for r0 in range(0, rows, 128):
        part = crow_ref[:, r0 : r0 + 128]
        part = jnp.concatenate([part, jnp.zeros((128 - heads, 128), F32)], axis=0)
        ccol_ref[r0 : r0 + 128, :] = part.T


def fill_bias(first, ends, bias_ref):
    for c in range(bias_ref.shape[0] // CHUNK):
        base = first + c * CHUNK
        t_pos = base + iota((CHUNK, 1), 0)
        start = run_start(ends, t_pos)
        s_pos = base + iota((CHUNK, CHUNK), 1)
        keep = (s_pos <= t_pos) & (s_pos >= start)
        bias_ref[c * CHUNK : (c + 1) * CHUNK, :] = jnp.where(keep, math.log2(SCALE), NEG)


def attend(first, ends, q_ref, k_ref, v_ref, h, crow_ref, ccol_ref, bias_ref, states, emit):
    rows = q_ref.shape[0]
    pair = range(2)
    half = CHUNK // 2
    lanes = [slice(i * 128, (i + 1) * 128) for i in pair]
    row_all = [crow_ref[pl.ds(h + i, 1), :] for i in pair]
    col_all = [head_column(ccol_ref, h + i) for i in pair]
    starts = range(0, rows, CHUNK)
    spans = [slice(r0, r0 + CHUNK) for r0 in starts]
    reach = [run_end(ends, first + r0 - 1) - (first + r0) for r0 in starts]
    base = [[row_all[i][:, r0 - 1 : r0] if r0 else jnp.zeros((1, 1), F32) for r0 in starts] for i in pair]

    fresh = [[], []]
    for c, r0 in enumerate(starts[:-1]):
        since = run_start(ends, first + r0 + CHUNK - 1) - (first + r0)
        inside = iota((1, CHUNK), 1) >= since
        for i in pair:
            row = row_all[i][:, spans[c]]
            weight = jnp.exp2(jnp.where(inside, row[:, CHUNK - 1 :] - row, NEG) + math.log2(SCALE))
            flipped = k_ref[spans[c], lanes[i]].T
            fresh[i].append(dot((flipped.astype(F32) * weight).astype(BF16), v_ref[spans[c], lanes[i]]))
    carried = []
    for i in pair:
        state, chain = states[i], [states[i].astype(BF16)]
        for c in range(len(starts) - 1):
            total = row_all[i][:, starts[c] + CHUNK - 1 : starts[c] + CHUNK]
            state = fresh[i][c] + state * jnp.exp2(jnp.where(CHUNK <= reach[c], total - base[i][c], NEG))
            chain.append(state.astype(BF16))
        carried.append(chain)

    def products(c):
        result = []
        for i in pair:
            query = q_ref[spans[c], lanes[i]]
            scores = dot(query, k_ref[spans[c], lanes[i]], ((1,), (1,)))
            result.append((scores, dot(query, carried[i][c])))
        return result

    ahead = products(0)
    for c, r0 in enumerate(starts):
        current = ahead
        if c + 1 < len(starts):
            ahead = products(c + 1)
        for part in range(2):
            t0, width = part * half, (part + 1) * half
            rows_here = slice(r0 + t0, r0 + t0 + half)
            for i in pair:
                scores, carry = current[i]
                col = col_all[i][rows_here]
                decay = jnp.exp2((col - row_all[i][:, r0 : r0 + width]) + bias_ref[rows_here, :width])
                weights = (scores[t0 : t0 + half, :width] * decay).astype(BF16)
                att = dot(weights, v_ref[r0 : r0 + width, lanes[i]])
                lead = jnp.exp2(jnp.where(t0 + iota((half, 1), 0) < reach[c], col - base[i][c], NEG))
                emit(lanes[i], r0 + t0, half, att + lead * carry[t0 : t0 + half])


def gather_last(refs, last_ref):
    me = lax.axis_index("seq") % MEMBERS
    for x, ref in enumerate(refs):
        last_ref[me ^ x] = ref[...]


def decay_of(last_ref, e, i, hp):
    extra = last_ref[e, hp * 128 :, :].astype(F32)
    return extra[i : i + 1, :] + extra[hp + i : hp + i + 1, :]


def scan_quad(rows, len_ref, last_ref, state, i, hp, note):
    members = last_ref.shape[0]
    ends = read_ends(len_ref, len_ref.shape[0])
    base = lax.axis_index("seq") // members * members
    for e in range(members):
        note(e, state)
        low = (base + e) * rows
        inner = jnp.int32(0)
        for end in ends:
            inner = inner + ((end > low) & (end < low + rows)).astype(jnp.int32)
        passes = (inner == 0).astype(F32)
        piece = last_ref[e, i * 128 : (i + 1) * 128, :].astype(F32)
        state = state * (decay_of(last_ref, e, i, hp) * passes) + piece
    return state


def leave_kernel(rows, len_ref, *refs):
    out_ref, last_ref = refs[-2:]
    gather_last(refs[:MEMBERS], last_ref)
    hp = out_ref.shape[0]
    for i in range(hp):
        state = jnp.zeros((128, 128), F32)
        if len(refs) > MEMBERS + 2:
            state = refs[MEMBERS][i].astype(F32)
        state = scan_quad(rows, len_ref, last_ref, state, i, hp, lambda e, x: None)
        out_ref[i] = state.astype(BF16)


def leave_quad(doc_lengths, last, coming, rows, hp):
    return pl.pallas_call(
        functools.partial(leave_kernel, rows),
        in_specs=[SMEM] + [VMEM] * (MEMBERS + len(coming)),
        out_specs=VMEM,
        out_shape=jax.ShapeDtypeStruct((hp, 128, 128), BF16),
        scratch_shapes=[pltpu.VMEM((MEMBERS,) + last[0].shape, BF16)],
        compiler_params=SMALL,
        name="leave_quad",
    )(doc_lengths, *last, *coming)


def enter_kernel(rows, len_ref, *refs):
    in_ref, out_refs, last_ref, state_ref = refs[MEMBERS], refs[MEMBERS + 1 : -2], refs[-2], refs[-1]
    gather_last(refs[:MEMBERS], last_ref)
    hp = in_ref.shape[0]

    def note(i, e, state):
        state_ref[e, i] = state

    for i in range(hp):
        scan_quad(rows, len_ref, last_ref, in_ref[i].astype(F32), i, hp, functools.partial(note, i))
    me = lax.axis_index("seq") % MEMBERS
    for x, out_ref in enumerate(out_refs):
        out_ref[...] = state_ref[me ^ x].astype(BF16)


def enter_states(doc_lengths, last, coming, rows):
    return pl.pallas_call(
        functools.partial(enter_kernel, rows),
        in_specs=[SMEM] + [VMEM] * (MEMBERS + 1),
        out_specs=[VMEM] * MEMBERS,
        out_shape=[jax.ShapeDtypeStruct(coming.shape, BF16)] * MEMBERS,
        scratch_shapes=[
            pltpu.VMEM((MEMBERS,) + last[0].shape, BF16),
            pltpu.VMEM((MEMBERS,) + coming.shape, F32),
        ],
        compiler_params=SMALL,
        name="enter_states",
    )(doc_lengths, *last, coming)


def final_kernel(rows, len_ref, own_ref, *refs):
    side_ref, in_ref, out_ref, last_ref, state_ref = refs[MEMBERS:]
    gather_last(refs[:MEMBERS], last_ref)
    hp = in_ref.shape[0]
    ends = read_ends(len_ref, len_ref.shape[0])
    base = lax.axis_index("seq") // MEMBERS * MEMBERS

    def note(i, e, state):
        state_ref[e, i] = state

    for i in range(hp):
        scan_quad(rows, len_ref, last_ref, in_ref[i].astype(F32), i, hp, functools.partial(note, i))
    out_ref[...] = jnp.zeros_like(out_ref)
    place, previous = jnp.int32(0), jnp.int32(-1)
    for d in range(len(ends)):
        device = (ends[d] - 1) // rows
        place = jnp.where(device == previous, place + 1, 0)
        previous = device
        at_end = ends[d] == (device + 1) * rows
        enters = (place == 0).astype(F32)
        mine = device // MEMBERS * MEMBERS == base
        e = device - base

        def put(i, local):
            state = local.astype(F32) + state_ref[e, i] * (decay_of(last_ref, e, i, hp) * enters)
            out_ref[own_ref[d], i] = state.astype(BF16)

        @pl.when(mine & at_end)
        def _():
            for i in range(hp):
                put(i, last_ref[e, i * 128 : (i + 1) * 128, :])

        @pl.when(mine & jnp.logical_not(at_end))
        def _():
            for i in range(hp):
                row = pl.multiple_of((jnp.minimum(place, SIDE - 1) * hp + i) * 128, 128)
                put(i, side_ref[e, pl.ds(row, 128), :])


def final_states(doc_lengths, owner_ids, last, side, coming, rows, spread):
    return pl.pallas_call(
        functools.partial(final_kernel, rows),
        in_specs=[SMEM, SMEM] + [VMEM] * (MEMBERS + 2),
        out_specs=VMEM,
        out_shape=jax.ShapeDtypeStruct((spread,) + coming.shape, BF16),
        scratch_shapes=[
            pltpu.VMEM((MEMBERS,) + last[0].shape, BF16),
            pltpu.VMEM((MEMBERS,) + coming.shape, F32),
        ],
        compiler_params=SMALL,
        name="final_states",
    )(doc_lengths, owner_ids, *last, side, coming)


def finish_kernel(len_ref, q_ref, k_ref, v_ref, e0, e1, e2, e3, gate_ref, gain_ref, crow_ref, out_ref, bias_ref, ccol_ref):
    rows = q_ref.shape[0]
    step = pl.program_id(0)
    me = lax.axis_index("seq")
    first = me * rows
    ends = read_ends(len_ref, len_ref.shape[0])
    hp = e0.shape[0]

    def entering(h):
        far = (h // hp) ^ (me % MEMBERS)
        state = e0[h % hp]
        for x, ref in ((1, e1), (2, e2), (3, e3)):
            state = jnp.where(far == x, ref[h % hp], state)
        return state

    def emit(lanes, t0, size, att):
        mean = jnp.mean(att * att, axis=1, keepdims=True)
        gate = 0.5 + 0.5 * jnp.tanh(0.5 * gate_ref[t0 : t0 + size, lanes].astype(F32))
        gain = gain_ref[:, lanes].astype(F32)
        out_ref[t0 : t0 + size, lanes] = (att * lax.rsqrt(mean + 1e-06) * (gain * gate)).astype(BF16)

    @pl.when(step == 0)
    def _():
        fill_bias(first, ends, bias_ref)
        fill_columns(crow_ref, ccol_ref)

    states = [entering(step * 2 + i).astype(F32) for i in range(2)]
    attend(first, ends, q_ref, k_ref, v_ref, step * 2, crow_ref, ccol_ref, bias_ref, states, emit)


def finish(doc_lengths, queries, keys, values, entering, gate, gain, crow):
    heads, rows = crow.shape
    wide = pl.BlockSpec((rows, 256), lambda j: (0, j))
    return pl.pallas_call(
        finish_kernel,
        grid=(heads // 2,),
        in_specs=[SMEM, wide, wide, wide]
        + [whole(e.shape) for e in entering]
        + [wide, pl.BlockSpec((1, 256), lambda j: (0, j)), whole((heads, rows))],
        out_specs=wide,
        out_shape=jax.ShapeDtypeStruct((rows, heads * 128), BF16),
        scratch_shapes=[pltpu.VMEM((rows, CHUNK), F32), pltpu.VMEM((rows, 128), F32)],
        compiler_params=pltpu.CompilerParams(vmem_limit_bytes=57 * 2**20),
        cost_estimate=pl.CostEstimate(
            flops=heads * rows * CHUNK * 128 * 8, bytes_accessed=rows * heads * 128 * 10, transcendentals=heads * rows * CHUNK
        ),
        name="finish",
    )(doc_lengths, queries, keys, values, *entering, gate, gain, crow)


def swap(x, groups=None):
    return lax.all_to_all(x, "seq", split_axis=0, concat_axis=0, axis_index_groups=groups, tiled=True)


def by_distance(parcels, spread):
    return [parcels[0]] + [
        lax.ppermute(parcels[x], "seq", [(s, s ^ x) for s in range(spread)]) for x in range(1, MEMBERS)
    ]


def on_device(spread, queries, keys, values, log_decay, gate, gain, doc_lengths, owner_ids):
    rows, heads = log_decay.shape
    quads = spread // MEMBERS
    hp = heads // MEMBERS
    near = [[q * MEMBERS + m for m in range(MEMBERS)] for q in range(quads)]
    onward = [(s, s + MEMBERS) for s in range(spread - MEMBERS)]
    decay_rows = log_decay.T
    barrier = lax.optimization_barrier

    side, crow, flags, *last = piece_states(doc_lengths, owner_ids, decay_rows, keys, values)
    side = swap(side, near)
    last = by_distance(last, spread)

    coming = []
    for _ in range(quads - 1):
        leaving = leave_quad(doc_lengths, last, coming, rows, hp)
        coming = [lax.ppermute(leaving, "seq", onward)]
    flags, gain, leaving = barrier((flags, gain, leaving))
    gain = gain.reshape(1, -1)

    def send_rest():
        rest, _ = piece_states(doc_lengths, owner_ids, decay_rows, keys, values, spread)
        return lax.dynamic_index_in_dim(swap(rest), flags[3], 0, True)

    rest = lax.cond(flags[2] > 0, send_rest, lambda: jnp.zeros((1, heads, 128, 128), BF16))
    from_quad = [flags[0] == q for q in range(1, quads)]
    coming, rest, gain, late, from_quad = barrier((coming[0], rest, gain, flags[1] > 0, from_quad))

    entering = by_distance(enter_states(doc_lengths, last, coming, rows), spread)
    finals = final_states(doc_lengths, owner_ids, last, side, coming, rows, spread)
    arrived = swap(finals).reshape(quads, 1, heads, 128, 128)
    entering, _ = barrier((entering, finals))
    mixed = finish(doc_lengths, queries, keys, values, entering, gate, gain, crow)
    owned = arrived[0]
    for q in range(1, quads):
        owned = jnp.where(from_quad[q - 1], arrived[q], owned)
    return mixed, jnp.where(late, rest, owned)


def solution(mesh):
    placed = (
        P(("groups", "seq"), "tp"),
        P(("groups", "seq"), "tp"),
        P(("groups", "seq"), "tp"),
        P(("groups", "seq"), "tp"),
        P(("groups", "seq"), "tp"),
        P("tp"),
        P("groups"),
        P("groups"),
    )
    return jax.shard_map(
        functools.partial(on_device, mesh.shape["seq"]),
        mesh=mesh,
        in_specs=placed,
        out_specs=(P(("groups", "seq"), "tp"), P(("groups", "seq"), "tp", None, None)),
        check_vma=False,
    )
```

profile of v0, /device:TPU:0, one launch (start us, length us, event | category | flops | bytes accessed | tf_op | source)
XLA Modules:
  0.0 101.5 jit_solution(3410627963476364301)
XLA Ops:
  0.6 0.0 copy-start.7
  0.6 0.0 copy-start.6
  0.7 0.0 copy-start.9
  0.7 9.2 %piece_states.3 = (bf16[4,1536,128]{2,1,0:T(8,128)(2,1)}, f32[16,1024]{1,0:T(8,128)}, s32[4]{0:T(128)S(1)}, bf16[528,128]{1,0:T(8,128)(2,1)}, bf16[528,128]{1,0:...) custom-call(s32[8]{0:T(128)} %len_ref.9, s32[8]{0:T(128)} %own_ref.3, f32[16,1024]{1,0:T(8,128)} %bitcast.9, ...), custom_call_target="tpu_custom_call" | custom-call | flops 2147483648 | bytes 8388608 | tf_op jit(solution)/shard_map/piece_states/pallas_call | solution.py:206
  9.9 3.0 %collective-permute-start = (bf16[528,128]{1,0:T(8,128)(2,1)}, bf16[528,128]{1,0:T(8,128)(2,1)S(1)}, u32[]{:S(2)}, u32[]{:S(2)}) collective-permute-start(bf16[528,128]{1,0:T(8,128)(2,1)} %get-tuple-element.47), channel_id=1, source_target_pairs={{0,2},{2,0},{4,6},{6,4},{8,10},{10,8},{12,14},{14,12},{1,3},{3,1},... | collective-permute-start | bytes 405512 | tf_op jit(solution)/shard_map/ppermute | solution.py:491
  12.9 1.6 %collective-permute-start.1 = (bf16[528,128]{1,0:T(8,128)(2,1)}, bf16[528,128]{1,0:T(8,128)(2,1)S(1)}, u32[]{:S(2)}, u32[]{:S(2)}) collective-permute-start(bf16[528,128]{1,0:T(8,128)(2,1)} %get-tuple-element.48), channel_id=1, source_target_pairs={{0,4},{2,6},{4,0},{6,2},{8,12},{10,14},{12,8},{14,10},{1,5},{3,7},... | collective-permute-start | bytes 405512 | tf_op jit(solution)/shard_map/ppermute | solution.py:491
  14.5 0.0 collective-permute-start.2
  14.5 2.2 %collective-permute-done.refs_1_ = bf16[528,128]{1,0:T(8,128)(2,1)S(1)} collective-permute-done((bf16[528,128]{1,0:T(8,128)(2,1)}, bf16[528,128]{1,0:T(8,128)(2,1)S(1)}, u32[]{:S(2)}, u32[]{:S(2)}) %collective-permute-start) | collective-permute-done | bytes 135200 | tf_op jit(solution)/shard_map/ppermute | solution.py:491
  16.7 2.9 %collective-permute-done.1.refs_2_ = bf16[528,128]{1,0:T(8,128)(2,1)S(1)} collective-permute-done((bf16[528,128]{1,0:T(8,128)(2,1)}, bf16[528,128]{1,0:T(8,128)(2,1)S(1)}, u32[]{:S(2)}, u32[]{:S(2)}) %collective-permute-start.1) | collective-permute-done | bytes 135200 | tf_op jit(solution)/shard_map/ppermute | solution.py:491
  19.7 1.2 %collective-permute-done.2.refs_3_ = bf16[528,128]{1,0:T(8,128)(2,1)S(1)} collective-permute-done((bf16[528,128]{1,0:T(8,128)(2,1)}, bf16[528,128]{1,0:T(8,128)(2,1)S(1)}, u32[]{:S(2)}, u32[]{:S(2)}) %collective-permute-start.2) | collective-permute-done | bytes 135200 | tf_op jit(solution)/shard_map/ppermute | solution.py:491
  20.9 0.0 copy-done.7
  20.9 0.0 copy-start
  20.9 0.9 copy-done
  21.8 0.7 leave_quad.1
  22.5 0.6 fusion
  23.8 0.0 copy-done.6
  23.8 0.0 copy-done.9
  23.9 0.0 copy-start.8
  23.9 0.0 copy-start.1
  23.9 0.1 conditional.1
  23.9 0.1 broadcast.12
  24.0 4.0 %all-to-all-start.1 = ((bf16[4,1536,128]{2,1,0:T(8,128)(2,1)}), bf16[4,1536,128]{2,1,0:T(8,128)(2,1)S(1)}, u32[]{:S(2)}, u32[]{:S(2)}) async-start(bf16[4,1536,128]{2,1,0:T(8,128)(2,1)} %get-tuple-element.58), calls=%async_computation.1 | async-start | bytes 3145728 | tf_op jit(solution)/shard_map/all_to_all | solution.py:486
  28.0 4.5 %collective-permute-start.3 = (bf16[4,128,128]{2,1,0:T(8,128)(2,1)S(1)}, bf16[4,128,128]{2,1,0:T(8,128)(2,1)S(1)}, u32[]{:S(2)}, u32[]{:S(2)}) collective-permute-start(bf16[4,128,128]{2,1,0:T(8,128)(2,1)S(1)} %leave_quad.1), channel_id=1, source_target_pairs={{0,8},{2,10},{4,12},{6,14},{1,9},{3,11},{5,13},{7,15},{16,24},{18,... | collective-permute-start | bytes 393224 | tf_op jit(solution)/shard_map/ppermute | solution.py:511
  32.5 0.0 copy-done.8
  32.5 0.6 reshape.42.gain_ref
  34.3 12.4 %collective-permute-done.3.refs_4_.refs_5_ = bf16[4,128,128]{2,1,0:T(8,128)(2,1)S(1)} collective-permute-done((bf16[4,128,128]{2,1,0:T(8,128)(2,1)S(1)}, bf16[4,128,128]{2,1,0:T(8,128)(2,1)S(1)}, u32[]{:S(2)}, u32[]{:S(2)}) %collective-permute-start.3) | collective-permute-done | bytes 131104 | tf_op jit(solution)/shard_map/ppermute | solution.py:511
  46.7 0.0 all-to-all-done.1.refs_4_
  46.7 0.0 copy-done.1
  46.7 2.1 %final_states.1 = bf16[8,4,128,128]{3,2,1,0:T(8,128)(2,1)} custom-call(s32[8]{0:T(128)S(1)} %copy-done.7, s32[8]{0:T(128)S(1)} %copy-done.9, bf16[528,128]{1,0:T(8,128)(2,1)S(1)} %copy-done.1, bf16[528,128]{1,0:T(8,128)(2,1)S(1)} %collective-permute-done.refs_1_, bf16[528,128]{1,0:T(8,128)(2,1)S(1)} %collective-permute-done.1.refs_2_, ...), custom_call_target="tpu_custom_call" | custom-call | tf_op jit(solution)/shard_map/final_states/pallas_call | solution.py:421
  48.8 7.5 %all-to-all-start.2 = ((bf16[8,4,128,128]{3,2,1,0:T(8,128)(2,1)}), bf16[8,4,128,128]{3,2,1,0:T(8,128)(2,1)S(1)}, u32[]{:S(2)}, u32[]{:S(2)}) async-start(bf16[8,4,128,128]{3,2,1,0:T(8,128)(2,1)} %final_states.1), calls=%async_computation.2 | async-start | bytes 2097152 | tf_op jit(solution)/shard_map/all_to_all | solution.py:486
  56.4 0.8 enter_states.1
  57.1 0.0 copy-start.2
  57.1 0.6 copy-done.2
  57.8 2.0 %collective-permute-start.4 = (bf16[4,128,128]{2,1,0:T(8,128)(2,1)S(1)}, bf16[4,128,128]{2,1,0:T(8,128)(2,1)S(1)}, u32[]{:S(2)}, u32[]{:S(2)}) collective-permute-start(bf16[4,128,128]{2,1,0:T(8,128)(2,1)S(1)} %get-tuple-element.55), channel_id=1, source_target_pairs={{0,2},{2,0},{4,6},{6,4},{8,10},{10,8},{12,14},{14,12},{1,3},{3,1},... | collective-permute-start | bytes 393224 | tf_op jit(solution)/shard_map/ppermute | solution.py:491
  59.8 1.5 %collective-permute-start.5 = (bf16[4,128,128]{2,1,0:T(8,128)(2,1)S(1)}, bf16[4,128,128]{2,1,0:T(8,128)(2,1)S(1)}, u32[]{:S(2)}, u32[]{:S(2)}) collective-permute-start(bf16[4,128,128]{2,1,0:T(8,128)(2,1)S(1)} %get-tuple-element.56), channel_id=1, source_target_pairs={{0,4},{2,6},{4,0},{6,2},{8,12},{10,14},{12,8},{14,10},{1,5},{3,7},... | collective-permute-start | bytes 393224 | tf_op jit(solution)/shard_map/ppermute | solution.py:491
  61.3 0.0 collective-permute-start.6
  61.3 4.8 %collective-permute-done.4.e1 = bf16[4,128,128]{2,1,0:T(8,128)(2,1)S(1)} collective-permute-done((bf16[4,128,128]{2,1,0:T(8,128)(2,1)S(1)}, bf16[4,128,128]{2,1,0:T(8,128)(2,1)S(1)}, u32[]{:S(2)}, u32[]{:S(2)}) %collective-permute-start.4) | collective-permute-done | bytes 131104 | tf_op jit(solution)/shard_map/ppermute | solution.py:491
  66.1 0.0 copy-start.3
  66.1 10.1 %collective-permute-done.5.e2 = bf16[4,128,128]{2,1,0:T(8,128)(2,1)S(1)} collective-permute-done((bf16[4,128,128]{2,1,0:T(8,128)(2,1)S(1)}, bf16[4,128,128]{2,1,0:T(8,128)(2,1)S(1)}, u32[]{:S(2)}, u32[]{:S(2)}) %collective-permute-start.5) | collective-permute-done | bytes 131104 | tf_op jit(solution)/shard_map/ppermute | solution.py:491
  76.1 0.0 copy-start.4
  76.1 2.5 %collective-permute-done.6.e3 = bf16[4,128,128]{2,1,0:T(8,128)(2,1)S(1)} collective-permute-done((bf16[4,128,128]{2,1,0:T(8,128)(2,1)S(1)}, bf16[4,128,128]{2,1,0:T(8,128)(2,1)S(1)}, u32[]{:S(2)}, u32[]{:S(2)}) %collective-permute-start.6) | collective-permute-done | bytes 131104 | tf_op jit(solution)/shard_map/ppermute | solution.py:491
  78.7 0.0 copy-done.3
  78.7 0.0 copy-done.4
  78.7 0.6 copy-done.5
  79.3 21.2 %finish.1 = bf16[1024,2048]{1,0:T(8,128)(2,1)} custom-call(s32[8]{0:T(128)S(1)} %copy-done.7, bf16[1024,2048]{1,0:T(8,128)(2,1)} %q_ref.1, bf16[1024,2048]{1,0:T(8,128)(2,1)} %k_ref.3, bf16[1024,2048]{1,0:T(8,128)(2,1)} %v_ref.3, bf16[4,128,128]{2,1,0:T(8,128)(2,1)} %copy-done.2, bf16[4,128,128]{2,1,0:T(8,128)(2,1)} %copy-done.3, ...), custom_call_target="tpu_custom_call" | custom-call | flops 4294967296 | bytes 20971520 | tf_op jit(solution)/shard_map/finish/pallas_call | solution.py:468
  100.5 0.0 all-to-all-done.2
  100.6 0.1 slice_select_fusion
  100.6 0.9 bitcast_select_fusion
  (1 shorter events, 0.0 us)
Async XLA Ops:
  0.6 20.3 %copy-start.7 = (s32[8]{0:T(128)S(1)}, s32[8]{0:T(128)}, u32[]{:S(2)}) copy-start(s32[8]{0:T(128)} %len_ref.9) | copy-start | bytes 100
  0.6 23.2 %copy-start.6 = (f32[1024,16]{0,1:T(8,128)S(1)}, f32[1024,16]{0,1:T(8,128)}, u32[]{:S(2)}) copy-start(f32[1024,16]{0,1:T(8,128)} %param.13) | copy-start | bytes 196612
  0.7 23.2 %copy-start.9 = (s32[8]{0:T(128)S(1)}, s32[8]{0:T(128)}, u32[]{:S(2)}) copy-start(s32[8]{0:T(128)} %own_ref.3) | copy-start | bytes 100
  9.9 6.8 %collective-permute-start = (bf16[528,128]{1,0:T(8,128)(2,1)}, bf16[528,128]{1,0:T(8,128)(2,1)S(1)}, u32[]{:S(2)}, u32[]{:S(2)}) collective-permute-start(bf16[528,128]{1,0:T(8,128)(2,1)} %get-tuple-element.47), channel_id=1, source_target_pairs={{0,2},{2,0},{4,6},{6,4},{8,10},{10,8},{12,14},{14,12},{1,3},{3,1},... | collective-permute-start | bytes 405512 | tf_op jit(solution)/shard_map/ppermute | solution.py:491
  12.9 6.7 %collective-permute-start.1 = (bf16[528,128]{1,0:T(8,128)(2,1)}, bf16[528,128]{1,0:T(8,128)(2,1)S(1)}, u32[]{:S(2)}, u32[]{:S(2)}) collective-permute-start(bf16[528,128]{1,0:T(8,128)(2,1)} %get-tuple-element.48), channel_id=1, source_target_pairs={{0,4},{2,6},{4,0},{6,2},{8,12},{10,14},{12,8},{14,10},{1,5},{3,7},... | collective-permute-start | bytes 405512 | tf_op jit(solution)/shard_map/ppermute | solution.py:491
  14.5 6.4 %collective-permute-start.2 = (bf16[528,128]{1,0:T(8,128)(2,1)}, bf16[528,128]{1,0:T(8,128)(2,1)S(1)}, u32[]{:S(2)}, u32[]{:S(2)}) collective-permute-start(bf16[528,128]{1,0:T(8,128)(2,1)} %get-tuple-element.49), channel_id=1, source_target_pairs={{0,6},{2,4},{4,2},{6,0},{8,14},{10,12},{12,10},{14,8},{1,7},{3,5},... | collective-permute-start | bytes 405512 | tf_op jit(solution)/shard_map/ppermute | solution.py:491
  20.9 0.9 copy-start
  23.9 8.6 %copy-start.8 = (bf16[2048]{0:T(1024)(128)(2,1)S(1)}, bf16[2048]{0:T(1024)(128)(2,1)}, u32[]{:S(2)}) copy-start(bf16[2048]{0:T(1024)(128)(2,1)} %param.15) | copy-start | bytes 12292
  23.9 22.9 %copy-start.1 = (bf16[528,128]{1,0:T(8,128)(2,1)S(1)}, bf16[528,128]{1,0:T(8,128)(2,1)}, u32[]{:S(2)}) copy-start(bf16[528,128]{1,0:T(8,128)(2,1)} %get-tuple-element.46.refs_0_) | copy-start | bytes 405508
  24.0 22.7 %all-to-all-start.1 = ((bf16[4,1536,128]{2,1,0:T(8,128)(2,1)}), bf16[4,1536,128]{2,1,0:T(8,128)(2,1)S(1)}, u32[]{:S(2)}, u32[]{:S(2)}) async-start(bf16[4,1536,128]{2,1,0:T(8,128)(2,1)} %get-tuple-element.58), calls=%async_computation.1 | async-start | bytes 3145728 | tf_op jit(solution)/shard_map/all_to_all | solution.py:486
  28.0 18.8 %collective-permute-start.3 = (bf16[4,128,128]{2,1,0:T(8,128)(2,1)S(1)}, bf16[4,128,128]{2,1,0:T(8,128)(2,1)S(1)}, u32[]{:S(2)}, u32[]{:S(2)}) collective-permute-start(bf16[4,128,128]{2,1,0:T(8,128)(2,1)S(1)} %leave_quad.1), channel_id=1, source_target_pairs={{0,8},{2,10},{4,12},{6,14},{1,9},{3,11},{5,13},{7,15},{16,24},{18,... | collective-permute-start | bytes 393224 | tf_op jit(solution)/shard_map/ppermute | solution.py:511
  48.8 51.7 %all-to-all-start.2 = ((bf16[8,4,128,128]{3,2,1,0:T(8,128)(2,1)}), bf16[8,4,128,128]{3,2,1,0:T(8,128)(2,1)S(1)}, u32[]{:S(2)}, u32[]{:S(2)}) async-start(bf16[8,4,128,128]{3,2,1,0:T(8,128)(2,1)} %final_states.1), calls=%async_computation.2 | async-start | bytes 2097152 | tf_op jit(solution)/shard_map/all_to_all | solution.py:486
  57.1 0.7 copy-start.2
  57.8 8.3 %collective-permute-start.4 = (bf16[4,128,128]{2,1,0:T(8,128)(2,1)S(1)}, bf16[4,128,128]{2,1,0:T(8,128)(2,1)S(1)}, u32[]{:S(2)}, u32[]{:S(2)}) collective-permute-start(bf16[4,128,128]{2,1,0:T(8,128)(2,1)S(1)} %get-tuple-element.55), channel_id=1, source_target_pairs={{0,2},{2,0},{4,6},{6,4},{8,10},{10,8},{12,14},{14,12},{1,3},{3,1},... | collective-permute-start | bytes 393224 | tf_op jit(solution)/shard_map/ppermute | solution.py:491
  59.8 16.3 %collective-permute-start.5 = (bf16[4,128,128]{2,1,0:T(8,128)(2,1)S(1)}, bf16[4,128,128]{2,1,0:T(8,128)(2,1)S(1)}, u32[]{:S(2)}, u32[]{:S(2)}) collective-permute-start(bf16[4,128,128]{2,1,0:T(8,128)(2,1)S(1)} %get-tuple-element.56), channel_id=1, source_target_pairs={{0,4},{2,6},{4,0},{6,2},{8,12},{10,14},{12,8},{14,10},{1,5},{3,7},... | collective-permute-start | bytes 393224 | tf_op jit(solution)/shard_map/ppermute | solution.py:491
  61.3 17.4 %collective-permute-start.6 = (bf16[4,128,128]{2,1,0:T(8,128)(2,1)S(1)}, bf16[4,128,128]{2,1,0:T(8,128)(2,1)S(1)}, u32[]{:S(2)}, u32[]{:S(2)}) collective-permute-start(bf16[4,128,128]{2,1,0:T(8,128)(2,1)S(1)} %get-tuple-element.57), channel_id=1, source_target_pairs={{0,6},{2,4},{4,2},{6,0},{8,14},{10,12},{12,10},{14,8},{1,7},{3,5},... | collective-permute-start | bytes 393224 | tf_op jit(solution)/shard_map/ppermute | solution.py:491
  66.1 12.6 %copy-start.3 = (bf16[4,128,128]{2,1,0:T(8,128)(2,1)}, bf16[4,128,128]{2,1,0:T(8,128)(2,1)S(1)}, u32[]{:S(2)}) copy-start(bf16[4,128,128]{2,1,0:T(8,128)(2,1)S(1)} %collective-permute-done.4.e1) | copy-start | bytes 393220
  76.1 2.5 %copy-start.4 = (bf16[4,128,128]{2,1,0:T(8,128)(2,1)}, bf16[4,128,128]{2,1,0:T(8,128)(2,1)S(1)}, u32[]{:S(2)}) copy-start(bf16[4,128,128]{2,1,0:T(8,128)(2,1)S(1)} %collective-permute-done.5.e2) | copy-start | bytes 393220
  78.7 0.6 copy-start.5
where the time goes:
time: 102 us; the launch traced here: 101 us
  waiting for transfers between devices  36.2 us (35%)
  Pallas kernels  34 us (33%)
  starting transfers between devices  24.1 us (24%)
  local copies, waits for them, and re-layouts  3.57 us (4%)
  between operations  2.69 us (3%)
    ppermute x6, waiting for transfers between devices, by_distance(): lax.ppermute(parcels[x], 'seq', [(s, s ^ x) for s in range(spread)])  23.8 us
    pallas_call x1, Pallas kernels, finish(): pl.pallas_call(finish_kernel, grid=(heads // 2,), in_specs=[SMEM, wide, w...  21.2 us
    ppermute x1, waiting for transfers between devices, on_device(): coming = [lax.ppermute(leaving, 'seq', onward)]  12.4 us
    all_to_all x2, starting transfers between devices, swap(): lax.all_to_all(x, 'seq', split_axis=0, concat_axis=0, axis_index_groups=g...  11.5 us
    pallas_call x1, Pallas kernels, piece_states(): pl.pallas_call(functools.partial(pieces_kernel, by_owner), grid=(heads //...  9.25 us
    ppermute x6, starting transfers between devices, by_distance(): lax.ppermute(parcels[x], 'seq', [(s, s ^ x) for s in range(spread)])  8.1 us
    ppermute x1, starting transfers between devices, on_device(): coming = [lax.ppermute(leaving, 'seq', onward)]  4.49 us
    unnamed x20, local copies, waits for them, and re-layouts  2.23 us
  transfers between devices with their start and end apart: 9, of which 7 were waited for; matrix products, arithmetic and copies ran while one was open for 1% of the time, Pallas kernels for 22%

commit v1 on v0

--- a/solution.py
+++ b/solution.py
@@ -10,6 +10,7 @@
 
 BLK = 512
 SIDE = 3
+SENT = (2, 1)
 EXTRA = 16
 CHUNK = 256
 MEMBERS = 4
@@ -94,9 +95,9 @@
     if by_owner:
         side_ref, crow_ref, w_ref, keep_ref = refs
     else:
-        side_ref, crow_ref, flag_ref = refs[:3]
-        last_refs = refs[3 : 3 + MEMBERS]
-        w_ref, keep_ref, first_ref = refs[3 + MEMBERS :]
+        side_refs, crow_ref, flag_ref = refs[:2], refs[2], refs[3]
+        last_refs = refs[4 : 4 + MEMBERS]
+        w_ref, keep_ref, first_ref = refs[4 + MEMBERS :]
     heads, rows = crow_ref.shape
     slots = keep_ref.shape[0]
     step = pl.program_id(0)
@@ -165,8 +166,9 @@
                 if by_owner:
                     side_ref[s, i + j] = state
                 elif s < SIDE:
-                    at = (s * hp + i + j) * 128
-                    side_ref[0, at : at + 128, :] = state
+                    part, slot = (0, s) if s < SENT[0] else (1, s - SENT[0])
+                    at = (slot * hp + i + j) * 128
+                    side_refs[part][0, at : at + 128, :] = state
                 else:
                     last_states.append(state)
     if not by_owner:
@@ -196,12 +198,13 @@
     else:
         last = (hp * 128 + EXTRA, 128)
         shapes = [
-            jax.ShapeDtypeStruct((MEMBERS, SIDE * hp * 128, 128), BF16),
+            *[jax.ShapeDtypeStruct((MEMBERS, n * hp * 128, 128), BF16) for n in SENT],
             jax.ShapeDtypeStruct((heads, rows), F32),
             jax.ShapeDtypeStruct((4,), jnp.int32),
-        ] + [jax.ShapeDtypeStruct(last, BF16)] * MEMBERS
-        specs = [pl.BlockSpec((1, SIDE * hp * 128, 128), lambda j: (j, 0, 0)), whole((heads, rows)), SMEM]
-        specs += [whole(last)] * MEMBERS
+            *[jax.ShapeDtypeStruct(last, BF16)] * MEMBERS,
+        ]
+        specs = [pl.BlockSpec((1, n * hp * 128, 128), lambda j: (j, 0, 0)) for n in SENT]
+        specs += [whole((heads, rows)), SMEM] + [whole(last)] * MEMBERS
         scratch.append(pltpu.VMEM((heads, 128), F32))
     return pl.pallas_call(
         functools.partial(pieces_kernel, by_owner),
@@ -379,7 +382,7 @@
 
 
 def final_kernel(rows, len_ref, own_ref, *refs):
-    side_ref, in_ref, out_ref, last_ref, state_ref = refs[MEMBERS:]
+    side1_ref, side2_ref, in_ref, out_ref, last_ref, state_ref = refs[MEMBERS:]
     gather_last(refs[:MEMBERS], last_ref)
     hp = in_ref.shape[0]
     ends = read_ends(len_ref, len_ref.shape[0])
@@ -410,17 +413,22 @@
             for i in range(hp):
                 put(i, last_ref[e, i * 128 : (i + 1) * 128, :])
 
-        @pl.when(mine & jnp.logical_not(at_end))
+        @pl.when(mine & jnp.logical_not(at_end) & (place < SENT[0]))
         def _():
             for i in range(hp):
-                row = pl.multiple_of((jnp.minimum(place, SIDE - 1) * hp + i) * 128, 128)
-                put(i, side_ref[e, pl.ds(row, 128), :])
+                put(i, side1_ref[e, pl.ds(pl.multiple_of((place * hp + i) * 128, 128), 128), :])
+
+        @pl.when(mine & jnp.logical_not(at_end) & (place >= SENT[0]))
+        def _():
+            slot = jnp.minimum(place - SENT[0], SENT[1] - 1)
+            for i in range(hp):
+                put(i, side2_ref[e, pl.ds(pl.multiple_of((slot * hp + i) * 128, 128), 128), :])
 
 
 def final_states(doc_lengths, owner_ids, last, side, coming, rows, spread):
     return pl.pallas_call(
         functools.partial(final_kernel, rows),
-        in_specs=[SMEM, SMEM] + [VMEM] * (MEMBERS + 2),
+        in_specs=[SMEM, SMEM] + [VMEM] * (MEMBERS + 3),
         out_specs=VMEM,
         out_shape=jax.ShapeDtypeStruct((spread,) + coming.shape, BF16),
         scratch_shapes=[
@@ -429,7 +437,7 @@
         ],
         compiler_params=SMALL,
         name="final_states",
-    )(doc_lengths, owner_ids, *last, side, coming)
+    )(doc_lengths, owner_ids, *last, *side, coming)
 
 
 def finish_kernel(len_ref, q_ref, k_ref, v_ref, e0, e1, e2, e3, gate_ref, gain_ref, crow_ref, out_ref, bias_ref, ccol_ref):
@@ -474,7 +482,7 @@
         out_specs=wide,
         out_shape=jax.ShapeDtypeStruct((rows, heads * 128), BF16),
         scratch_shapes=[pltpu.VMEM((rows, CHUNK), F32), pltpu.VMEM((rows, 128), F32)],
-        compiler_params=pltpu.CompilerParams(vmem_limit_bytes=57 * 2**20),
+        compiler_params=pltpu.CompilerParams(vmem_limit_bytes=54 * 2**20),
         cost_estimate=pl.CostEstimate(
             flops=heads * rows * CHUNK * 128 * 8, bytes_accessed=rows * heads * 128 * 10, transcendentals=heads * rows * CHUNK
         ),
@@ -501,9 +509,12 @@
     decay_rows = log_decay.T
     barrier = lax.optimization_barrier
 
-    side, crow, flags, *last = piece_states(doc_lengths, owner_ids, decay_rows, keys, values)
-    side = swap(side, near)
+    side1, side2, crow, flags, *last = piece_states(doc_lengths, owner_ids, decay_rows, keys, values)
     last = by_distance(last, spread)
+    side1, last[1] = barrier((side1, last[1]))
+    side1 = swap(side1, near)
+    side2, side1 = barrier((side2, side1))
+    side2 = swap(side2, near)
 
     coming = []
     for _ in range(quads - 1):
@@ -521,9 +532,9 @@
     coming, rest, gain, late, from_quad = barrier((coming[0], rest, gain, flags[1] > 0, from_quad))
 
     entering = by_distance(enter_states(doc_lengths, last, coming, rows), spread)
-    finals = final_states(doc_lengths, owner_ids, last, side, coming, rows, spread)
+    finals = final_states(doc_lengths, owner_ids, last, [side1, side2], coming, rows, spread)
+    entering, finals = barrier((entering, finals))
     arrived = swap(finals).reshape(quads, 1, heads, 128, 128)
-    entering, _ = barrier((entering, finals))
     mixed = finish(doc_lengths, queries, keys, values, entering, gate, gain, crow)
     owned = arrived[0]
     for q in range(1, quads):

time: 102 us -> 92.1 us (0.903)
  waiting for transfers between devices: 36.2 us -> 10.6 us
  blocking collectives: 0 us -> 16.4 us
  starting transfers between devices: 24.1 us -> 22.9 us
    all_to_all x0 -> x1, blocking collectives: none -> 16.4 us  [swap(): lax.all_to_all(x, 'seq', split_axis=0, concat_axis=0, axis_index_groups=g...]
    ppermute x6, waiting for transfers between devices: 23.8 us -> 9.99 us  [by_distance(): lax.ppermute(parcels[x], 'seq', [(s, s ^ x) for s in range(spread)])]
    ppermute x1, waiting for transfers between devices: 12.4 us -> 0.55 us  [on_device(): coming = [lax.ppermute(leaving, 'seq', onward)]]
    all_to_all x2, starting transfers between devices: 11.5 us -> 8.99 us  [swap(): lax.all_to_all(x, 'seq', split_axis=0, concat_axis=0, axis_index_groups=g...]
    ppermute x6, starting transfers between devices: 8.1 us -> 9.42 us  [by_distance(): lax.ppermute(parcels[x], 'seq', [(s, s ^ x) for s in range(spread)])]
    unnamed x20 -> x22, local copies, waits for them, and re-layouts: 2.23 us -> 2.65 us
  transfers between devices with their start and end apart: 9 -> 9, of which waited for: 7 -> 6; matrix products, arithmetic and copies ran while one was open for 1% -> 1% of each run, Pallas kernels for 22% -> 26%
where the time goes in v1:
time: 92.1 us; the launch traced here: 91.7 us
  Pallas kernels  34.1 us (37%)
  starting transfers between devices  22.9 us (25%)
  blocking collectives  16.4 us (18%)
  waiting for transfers between devices  10.6 us (12%)
  local copies, waits for them, and re-layouts  4.01 us (4%)
  between operations  2.78 us (3%)
    pallas_call x1, Pallas kernels, finish(): pl.pallas_call(finish_kernel, grid=(heads // 2,), in_specs=[SMEM, wide, w...  21.2 us
    all_to_all x1, blocking collectives, swap(): lax.all_to_all(x, 'seq', split_axis=0, concat_axis=0, axis_index_groups=g...  16.4 us
    ppermute x6, waiting for transfers between devices, by_distance(): lax.ppermute(parcels[x], 'seq', [(s, s ^ x) for s in range(spread)])  9.99 us
    ppermute x6, starting transfers between devices, by_distance(): lax.ppermute(parcels[x], 'seq', [(s, s ^ x) for s in range(spread)])  9.42 us
    pallas_call x1, Pallas kernels, piece_states(): pl.pallas_call(functools.partial(pieces_kernel, by_owner), grid=(heads //...  9.22 us
    all_to_all x2, starting transfers between devices, swap(): lax.all_to_all(x, 'seq', split_axis=0, concat_axis=0, axis_index_groups=g...  8.99 us
    ppermute x1, starting transfers between devices, on_device(): coming = [lax.ppermute(leaving, 'seq', onward)]  4.5 us
    unnamed x22, local copies, waits for them, and re-layouts  2.65 us
  transfers between devices with their start and end apart: 9, of which 6 were waited for; matrix products, arithmetic and copies ran while one was open for 1% of the time, Pallas kernels for 26%

profile of v1, /device:TPU:0, one launch (start us, length us, event | category | flops | bytes accessed | tf_op | source)
XLA Modules:
  0.0 91.7 jit_solution(14242552543203450634)
XLA Ops:
  0.6 0.0 copy-start.8
  0.6 0.0 copy-start.7
  0.7 0.0 copy-start.10
  0.7 9.2 %piece_states.3 = (bf16[4,1024,128]{2,1,0:T(8,128)(2,1)}, bf16[4,512,128]{2,1,0:T(8,128)(2,1)}, f32[16,1024]{1,0:T(8,128)}, s32[4]{0:T(128)S(1)}, bf16[528,128]{...) custom-call(s32[8]{0:T(128)} %len_ref.9, s32[8]{0:T(128)} %own_ref.3, ...), custom_call_target="tpu_custom_call" | custom-call | flops 2147483648 | bytes 8388608 | tf_op jit(solution)/shard_map/piece_states/pallas_call | solution.py:209
  9.9 3.0 %collective-permute-start = (bf16[528,128]{1,0:T(8,128)(2,1)}, bf16[528,128]{1,0:T(8,128)(2,1)S(1)}, u32[]{:S(2)}, u32[]{:S(2)}) collective-permute-start(bf16[528,128]{1,0:T(8,128)(2,1)} %get-tuple-element.54), channel_id=1, source_target_pairs={{0,2},{2,0},{4,6},{6,4},{8,10},{10,8},{12,14},{14,12},{1,3},{3,1},... | collective-permute-start | bytes 405512 | tf_op jit(solution)/shard_map/ppermute | solution.py:499
  12.9 1.6 %collective-permute-start.1 = (bf16[528,128]{1,0:T(8,128)(2,1)}, bf16[528,128]{1,0:T(8,128)(2,1)S(1)}, u32[]{:S(2)}, u32[]{:S(2)}) collective-permute-start(bf16[528,128]{1,0:T(8,128)(2,1)} %get-tuple-element.56), channel_id=1, source_target_pairs={{0,4},{2,6},{4,0},{6,2},{8,12},{10,14},{12,8},{14,10},{1,5},{3,7},... | collective-permute-start | bytes 405512 | tf_op jit(solution)/shard_map/ppermute | solution.py:499
  14.5 0.0 collective-permute-start.2
  14.5 2.2 %collective-permute-done.refs_1_ = bf16[528,128]{1,0:T(8,128)(2,1)S(1)} collective-permute-done((bf16[528,128]{1,0:T(8,128)(2,1)}, bf16[528,128]{1,0:T(8,128)(2,1)S(1)}, u32[]{:S(2)}, u32[]{:S(2)}) %collective-permute-start) | collective-permute-done | bytes 135200 | tf_op jit(solution)/shard_map/ppermute | solution.py:499
  16.7 2.9 %collective-permute-done.1.refs_2_ = bf16[528,128]{1,0:T(8,128)(2,1)S(1)} collective-permute-done((bf16[528,128]{1,0:T(8,128)(2,1)}, bf16[528,128]{1,0:T(8,128)(2,1)S(1)}, u32[]{:S(2)}, u32[]{:S(2)}) %collective-permute-start.1) | collective-permute-done | bytes 135200 | tf_op jit(solution)/shard_map/ppermute | solution.py:499
  19.6 1.2 %collective-permute-done.2.refs_3_ = bf16[528,128]{1,0:T(8,128)(2,1)S(1)} collective-permute-done((bf16[528,128]{1,0:T(8,128)(2,1)}, bf16[528,128]{1,0:T(8,128)(2,1)S(1)}, u32[]{:S(2)}, u32[]{:S(2)}) %collective-permute-start.2) | collective-permute-done | bytes 135200 | tf_op jit(solution)/shard_map/ppermute | solution.py:499
  20.9 0.0 copy-done.8
  20.9 0.9 copy-done
  21.8 0.7 leave_quad.1
  22.5 0.7 fusion
  23.8 0.0 copy-done.7
  23.8 0.0 copy-done.10
  23.8 0.0 copy-start.3
  23.9 0.0 copy-start.9
  23.9 0.0 copy-start.1
  23.9 0.1 conditional.1
  23.9 0.1 broadcast.12
  24.0 1.1 %copy-done.3 = bf16[4,1024,128]{2,1,0:T(8,128)(2,1)S(1)} copy-done((bf16[4,1024,128]{2,1,0:T(8,128)(2,1)S(1)}, bf16[4,1024,128]{2,1,0:T(8,128)(2,1)}, u32[]{:S(2)}) %copy-start.3) | copy-done | bytes 1048600
  25.1 16.4 %all_to_all.19.refs_4_ = bf16[4,1024,128]{2,1,0:T(8,128)(2,1)S(1)} all-to-all(bf16[4,1024,128]{2,1,0:T(8,128)(2,1)S(1)} %copy-done.3), channel_id=1, replica_groups={{0,2,4,6},{8,10,12,14},{1,3,5,7},{9,11,13,15},{16,18,20,22},{24,26,28,3..., dimensions={0} | all-to-all | bytes 2097152 | tf_op jit(solution)/shard_map/all_to_all | solution.py:494
  41.5 3.5 %all-to-all-start.2 = ((bf16[4,512,128]{2,1,0:T(8,128)(2,1)}), bf16[4,512,128]{2,1,0:T(8,128)(2,1)S(1)}, u32[]{:S(2)}, u32[]{:S(2)}) async-start(bf16[4,512,128]{2,1,0:T(8,128)(2,1)} %get-tuple-element.69), calls=%async_computation.2 | async-start | bytes 1048576 | tf_op jit(solution)/shard_map/all_to_all | solution.py:494
  44.9 4.5 %collective-permute-start.3 = (bf16[4,128,128]{2,1,0:T(8,128)(2,1)S(1)}, bf16[4,128,128]{2,1,0:T(8,128)(2,1)S(1)}, u32[]{:S(2)}, u32[]{:S(2)}) collective-permute-start(bf16[4,128,128]{2,1,0:T(8,128)(2,1)S(1)} %leave_quad.1), channel_id=1, source_target_pairs={{0,8},{2,10},{4,12},{6,14},{1,9},{3,11},{5,13},{7,15},{16,24},{18,... | collective-permute-start | bytes 393224 | tf_op jit(solution)/shard_map/ppermute | solution.py:522
  49.4 0.0 copy-done.9
  49.5 0.6 reshape.42.gain_ref
  51.4 0.6 collective-permute-done.3.refs_4_.refs_6_
  51.9 0.0 copy-done.1
  51.9 0.8 enter_states.1
  52.7 0.0 copy-start.2
  52.7 0.6 copy-done.2
  53.3 2.0 %collective-permute-start.4 = (bf16[4,128,128]{2,1,0:T(8,128)(2,1)S(1)}, bf16[4,128,128]{2,1,0:T(8,128)(2,1)S(1)}, u32[]{:S(2)}, u32[]{:S(2)}) collective-permute-start(bf16[4,128,128]{2,1,0:T(8,128)(2,1)S(1)} %get-tuple-element.63), channel_id=1, source_target_pairs={{0,2},{2,0},{4,6},{6,4},{8,10},{10,8},{12,14},{14,12},{1,3},{3,1},... | collective-permute-start | bytes 393224 | tf_op jit(solution)/shard_map/ppermute | solution.py:499
  55.3 2.8 %collective-permute-start.5 = (bf16[4,128,128]{2,1,0:T(8,128)(2,1)S(1)}, bf16[4,128,128]{2,1,0:T(8,128)(2,1)S(1)}, u32[]{:S(2)}, u32[]{:S(2)}) collective-permute-start(bf16[4,128,128]{2,1,0:T(8,128)(2,1)S(1)} %get-tuple-element.64), channel_id=1, source_target_pairs={{0,4},{2,6},{4,0},{6,2},{8,12},{10,14},{12,8},{14,10},{1,5},{3,7},... | collective-permute-start | bytes 393224 | tf_op jit(solution)/shard_map/ppermute | solution.py:499
  58.2 0.0 collective-permute-start.6
  58.2 0.0 all-to-all-done.2.refs_5_
  58.2 2.2 %final_states.1 = bf16[8,4,128,128]{3,2,1,0:T(8,128)(2,1)} custom-call(s32[8]{0:T(128)} %len_ref.9, s32[8]{0:T(128)} %own_ref.3, bf16[528,128]{1,0:T(8,128)(2,1)S(1)} %copy-done.1, bf16[528,128]{1,0:T(8,128)(2,1)S(1)} %collective-permute-done.refs_1_, bf16[528,128]{1,0:T(8,128)(2,1)S(1)} %collective-permute-done.1.refs_2_, ...), custom_call_target="tpu_custom_call" | custom-call | tf_op jit(solution)/shard_map/final_states/pallas_call | solution.py:429
  60.4 0.0 collective-permute-done.4.e1
  60.4 0.7 collective-permute-done.5.e2
  61.1 2.9 %collective-permute-done.6.e3 = bf16[4,128,128]{2,1,0:T(8,128)(2,1)S(1)} collective-permute-done((bf16[4,128,128]{2,1,0:T(8,128)(2,1)S(1)}, bf16[4,128,128]{2,1,0:T(8,128)(2,1)S(1)}, u32[]{:S(2)}, u32[]{:S(2)}) %collective-permute-start.6) | collective-permute-done | bytes 131104 | tf_op jit(solution)/shard_map/ppermute | solution.py:499
  64.0 5.5 %all-to-all-start.3 = ((bf16[8,4,128,128]{3,2,1,0:T(8,128)(2,1)}), bf16[8,4,128,128]{3,2,1,0:T(8,128)(2,1)S(1)}, u32[]{:S(2)}, u32[]{:S(2)}) async-start(bf16[8,4,128,128]{3,2,1,0:T(8,128)(2,1)} %final_states.1), calls=%async_computation.3 | async-start | bytes 2097152 | tf_op jit(solution)/shard_map/all_to_all | solution.py:494
  69.5 0.0 copy-done.4
  69.5 0.0 copy-done.5
  69.6 0.0 copy-done.6
  69.6 21.2 %finish.1 = bf16[1024,2048]{1,0:T(8,128)(2,1)} custom-call(s32[8]{0:T(128)} %len_ref.9, bf16[1024,2048]{1,0:T(8,128)(2,1)} %q_ref.1, bf16[1024,2048]{1,0:T(8,128)(2,1)} %k_ref.3, bf16[1024,2048]{1,0:T(8,128)(2,1)} %v_ref.3, bf16[4,128,128]{2,1,0:T(8,128)(2,1)} %copy-done.2, bf16[4,128,128]{2,1,0:T(8,128)(2,1)} %copy-done.4, bf16[4,128,128]{2,1,0:T(8,128)(2,1)} %copy-done.5, ...), custom_call_target="tpu_custom_call" | custom-call | flops 4294967296 | bytes 20971520 | tf_op jit(solution)/shard_map/finish/pallas_call | solution.py:476
  90.8 0.0 all-to-all-done.3
  90.8 0.1 slice_select_fusion
  90.8 0.9 bitcast_select_fusion
  (4 shorter events, 0.0 us)
Async XLA Ops:
  0.6 20.3 %copy-start.8 = (s32[8]{0:T(128)S(1)}, s32[8]{0:T(128)}, u32[]{:S(2)}) copy-start(s32[8]{0:T(128)} %len_ref.9) | copy-start | bytes 100
  0.6 23.2 %copy-start.7 = (f32[1024,16]{0,1:T(8,128)S(1)}, f32[1024,16]{0,1:T(8,128)}, u32[]{:S(2)}) copy-start(f32[1024,16]{0,1:T(8,128)} %param.13) | copy-start | bytes 196612
  0.7 23.2 %copy-start.10 = (s32[8]{0:T(128)S(1)}, s32[8]{0:T(128)}, u32[]{:S(2)}) copy-start(s32[8]{0:T(128)} %own_ref.3) | copy-start | bytes 100
  9.9 6.8 %collective-permute-start = (bf16[528,128]{1,0:T(8,128)(2,1)}, bf16[528,128]{1,0:T(8,128)(2,1)S(1)}, u32[]{:S(2)}, u32[]{:S(2)}) collective-permute-start(bf16[528,128]{1,0:T(8,128)(2,1)} %get-tuple-element.54), channel_id=1, source_target_pairs={{0,2},{2,0},{4,6},{6,4},{8,10},{10,8},{12,14},{14,12},{1,3},{3,1},... | collective-permute-start | bytes 405512 | tf_op jit(solution)/shard_map/ppermute | solution.py:499
  12.9 6.7 %collective-permute-start.1 = (bf16[528,128]{1,0:T(8,128)(2,1)}, bf16[528,128]{1,0:T(8,128)(2,1)S(1)}, u32[]{:S(2)}, u32[]{:S(2)}) collective-permute-start(bf16[528,128]{1,0:T(8,128)(2,1)} %get-tuple-element.56), channel_id=1, source_target_pairs={{0,4},{2,6},{4,0},{6,2},{8,12},{10,14},{12,8},{14,10},{1,5},{3,7},... | collective-permute-start | bytes 405512 | tf_op jit(solution)/shard_map/ppermute | solution.py:499
  14.5 6.4 %collective-permute-start.2 = (bf16[528,128]{1,0:T(8,128)(2,1)}, bf16[528,128]{1,0:T(8,128)(2,1)S(1)}, u32[]{:S(2)}, u32[]{:S(2)}) collective-permute-start(bf16[528,128]{1,0:T(8,128)(2,1)} %get-tuple-element.57), channel_id=1, source_target_pairs={{0,6},{2,4},{4,2},{6,0},{8,14},{10,12},{12,10},{14,8},{1,7},{3,5},... | collective-permute-start | bytes 405512 | tf_op jit(solution)/shard_map/ppermute | solution.py:499
  20.9 0.9 copy-start
  23.8 1.2 %copy-start.3 = (bf16[4,1024,128]{2,1,0:T(8,128)(2,1)S(1)}, bf16[4,1024,128]{2,1,0:T(8,128)(2,1)}, u32[]{:S(2)}) copy-start(bf16[4,1024,128]{2,1,0:T(8,128)(2,1)} %get-tuple-element.67) | copy-start | bytes 3145732
  23.9 25.6 %copy-start.9 = (bf16[2048]{0:T(1024)(128)(2,1)S(1)}, bf16[2048]{0:T(1024)(128)(2,1)}, u32[]{:S(2)}) copy-start(bf16[2048]{0:T(1024)(128)(2,1)} %param.15) | copy-start | bytes 12292
  23.9 28.1 %copy-start.1 = (bf16[528,128]{1,0:T(8,128)(2,1)S(1)}, bf16[528,128]{1,0:T(8,128)(2,1)}, u32[]{:S(2)}) copy-start(bf16[528,128]{1,0:T(8,128)(2,1)} %get-tuple-element.52.refs_0_) | copy-start | bytes 405508
  41.5 16.7 %all-to-all-start.2 = ((bf16[4,512,128]{2,1,0:T(8,128)(2,1)}), bf16[4,512,128]{2,1,0:T(8,128)(2,1)S(1)}, u32[]{:S(2)}, u32[]{:S(2)}) async-start(bf16[4,512,128]{2,1,0:T(8,128)(2,1)} %get-tuple-element.69), calls=%async_computation.2 | async-start | bytes 1048576 | tf_op jit(solution)/shard_map/all_to_all | solution.py:494
  44.9 7.0 %collective-permute-start.3 = (bf16[4,128,128]{2,1,0:T(8,128)(2,1)S(1)}, bf16[4,128,128]{2,1,0:T(8,128)(2,1)S(1)}, u32[]{:S(2)}, u32[]{:S(2)}) collective-permute-start(bf16[4,128,128]{2,1,0:T(8,128)(2,1)S(1)} %leave_quad.1), channel_id=1, source_target_pairs={{0,8},{2,10},{4,12},{6,14},{1,9},{3,11},{5,13},{7,15},{16,24},{18,... | collective-permute-start | bytes 393224 | tf_op jit(solution)/shard_map/ppermute | solution.py:522
  52.7 0.6 copy-start.2
  53.3 7.1 %collective-permute-start.4 = (bf16[4,128,128]{2,1,0:T(8,128)(2,1)S(1)}, bf16[4,128,128]{2,1,0:T(8,128)(2,1)S(1)}, u32[]{:S(2)}, u32[]{:S(2)}) collective-permute-start(bf16[4,128,128]{2,1,0:T(8,128)(2,1)S(1)} %get-tuple-element.63), channel_id=1, source_target_pairs={{0,2},{2,0},{4,6},{6,4},{8,10},{10,8},{12,14},{14,12},{1,3},{3,1},... | collective-permute-start | bytes 393224 | tf_op jit(solution)/shard_map/ppermute | solution.py:499
  55.3 5.8 %collective-permute-start.5 = (bf16[4,128,128]{2,1,0:T(8,128)(2,1)S(1)}, bf16[4,128,128]{2,1,0:T(8,128)(2,1)S(1)}, u32[]{:S(2)}, u32[]{:S(2)}) collective-permute-start(bf16[4,128,128]{2,1,0:T(8,128)(2,1)S(1)} %get-tuple-element.64), channel_id=1, source_target_pairs={{0,4},{2,6},{4,0},{6,2},{8,12},{10,14},{12,8},{14,10},{1,5},{3,7},... | collective-permute-start | bytes 393224 | tf_op jit(solution)/shard_map/ppermute | solution.py:499
  58.2 5.9 %collective-permute-start.6 = (bf16[4,128,128]{2,1,0:T(8,128)(2,1)S(1)}, bf16[4,128,128]{2,1,0:T(8,128)(2,1)S(1)}, u32[]{:S(2)}, u32[]{:S(2)}) collective-permute-start(bf16[4,128,128]{2,1,0:T(8,128)(2,1)S(1)} %get-tuple-element.65), channel_id=1, source_target_pairs={{0,6},{2,4},{4,2},{6,0},{8,14},{10,12},{12,10},{14,8},{1,7},{3,5},... | collective-permute-start | bytes 393224 | tf_op jit(solution)/shard_map/ppermute | solution.py:499
  60.4 9.1 %copy-start.4 = (bf16[4,128,128]{2,1,0:T(8,128)(2,1)}, bf16[4,128,128]{2,1,0:T(8,128)(2,1)S(1)}, u32[]{:S(2)}) copy-start(bf16[4,128,128]{2,1,0:T(8,128)(2,1)S(1)} %collective-permute-done.4.e1) | copy-start | bytes 393220
  61.1 8.4 %copy-start.5 = (bf16[4,128,128]{2,1,0:T(8,128)(2,1)}, bf16[4,128,128]{2,1,0:T(8,128)(2,1)S(1)}, u32[]{:S(2)}) copy-start(bf16[4,128,128]{2,1,0:T(8,128)(2,1)S(1)} %collective-permute-done.5.e2) | copy-start | bytes 393220
  64.0 5.5 %copy-start.6 = (bf16[4,128,128]{2,1,0:T(8,128)(2,1)}, bf16[4,128,128]{2,1,0:T(8,128)(2,1)S(1)}, u32[]{:S(2)}) copy-start(bf16[4,128,128]{2,1,0:T(8,128)(2,1)S(1)} %collective-permute-done.6.e3) | copy-start | bytes 393220
  64.0 26.7 %all-to-all-start.3 = ((bf16[8,4,128,128]{3,2,1,0:T(8,128)(2,1)}), bf16[8,4,128,128]{3,2,1,0:T(8,128)(2,1)S(1)}, u32[]{:S(2)}, u32[]{:S(2)}) async-start(bf16[8,4,128,128]{3,2,1,0:T(8,128)(2,1)} %final_states.1), calls=%async_computation.3 | async-start | bytes 2097152 | tf_op jit(solution)/shard_map/all_to_all | solution.py:494
